TPU v7x, 128 devices: a whole 4x4x4 slice. The times are simulated.
128 devices in a mesh: row: 16 (over y_lo, z, core), col: 8 (over y_hi, x).
Axes of the slice: x: 4, y: 4 (y_hi: 2, y_lo: 2; y = y_hi * 2 + y_lo), z: 4, core: 2. Of those that a mesh axis runs over, the one named last changes fastest.
Arguments:
- grad_out: float32 [16, 512, 2048], P(None, 'row', 'col'), may hold values from -6 to 6
- input_spectrum: float32 [2, 16, 1024, 2048], P(None, None, ('row', 'col')), may hold values from -6 to 6
- filter_spectrum: float32 [2, 16, 1024, 2048], P(None, None, ('row', 'col')), may hold values from -6 to 6
Outputs:
- grad_input: float32 [16, 512, 2048], P(None, 'row', 'col')
- grad_filter: float32 [16, 512, 2048], P(None, 'row', 'col')
All inputs are finite; a program needn't handle non-finite values.
Results may differ from a plain program's by a relative error of at most 0.00007.
Values sent between devices are 32-bit elements; how exact they have to be, the bound alone decides.
A program may use at most 192 MiB of HBM per device.

v0:
```python
import math

import jax
import jax.numpy as jnp
from jax import lax
from jax.sharding import PartitionSpec as P

exact_prec = lax.Precision.HIGHEST


def cos_sin(index_a, index_b, period):
    phase_idx = index_a[:, None] * index_b[None, :] % period
    angle_val = phase_idx.astype(jnp.float32) * (2.0 * math.pi / period)
    return (jnp.cos(angle_val), jnp.sin(angle_val))


def split_order(count, col_size, block_len, stride):
    position = lax.iota(jnp.int32, count)
    group_idx = position // block_len
    inner_idx = position % block_len
    return group_idx % col_size * stride + group_idx // col_size * block_len + inner_idx


def forward_table(values, table):
    return jnp.einsum("...n,nq->...q", values, table, precision=exact_prec)


def backward_table(values, table):
    return jnp.einsum("...q,nq->...n", values, table, precision=exact_prec)


def local(grad_out, input_spectrum, filter_spectrum):
    row_size = lax.axis_size("row")
    col_size = lax.axis_size("col")
    row_pos = lax.axis_index("row")
    col_pos = lax.axis_index("col")
    n2_local = grad_out.shape[2]
    half_one = grad_out.shape[1] * row_size
    first_len = 2 * half_one
    second_len = n2_local * col_size
    total_len = first_len * second_len
    part_len = second_len // (row_size * col_size)
    k1_local = input_spectrum.shape[2]
    arranged = lax.all_to_all(grad_out, "row", split_axis=2, concat_axis=1, tiled=True)
    own_n2 = col_pos * n2_local + row_pos * part_len + lax.iota(jnp.int32, part_len)
    k1_all = lax.iota(jnp.int32, first_len)
    n1_all = lax.iota(jnp.int32, half_one)
    cos_one, sin_one = cos_sin(n1_all, k1_all, first_len)
    real_b = jnp.einsum("cnm,nk->ckm", arranged, cos_one, precision=exact_prec)
    imag_b = -jnp.einsum("cnm,nk->ckm", arranged, sin_one, precision=exact_prec)
    tw_cos, tw_sin = cos_sin(k1_all, own_n2, total_len)
    twisted = jnp.stack([real_b * tw_cos + imag_b * tw_sin, imag_b * tw_cos - real_b * tw_sin])
    own_k1 = (row_pos * col_size + col_pos) * k1_local + lax.iota(jnp.int32, k1_local)
    k2_all = lax.iota(jnp.int32, second_len)
    back_n2 = split_order(second_len, col_size, part_len, n2_local)
    moved = lax.all_to_all(twisted, ("row", "col"), split_axis=2, concat_axis=3, tiled=True)
    cos_two, sin_two = cos_sin(back_n2, k2_all, second_len)
    cos_back, sin_back = (cos_two, sin_two)
    up_real = forward_table(moved[0], cos_two) + forward_table(moved[1], sin_two)
    up_imag = forward_table(moved[1], cos_two) - forward_table(moved[0], sin_two)
    in_real = input_spectrum[0]
    in_imag = input_spectrum[1]
    fil_real = filter_spectrum[0]
    fil_imag = filter_spectrum[1]
    grad_real = jnp.stack(
        [up_real * fil_real + up_imag * fil_imag, up_real * in_real + up_imag * in_imag]
    )
    grad_imag = jnp.stack(
        [up_imag * fil_real - up_real * fil_imag, up_imag * in_real - up_real * in_imag]
    )
    back_real = backward_table(grad_real, cos_back) - backward_table(grad_imag, sin_back)
    back_imag = backward_table(grad_imag, cos_back) + backward_table(grad_real, sin_back)
    tb_cos, tb_sin = cos_sin(own_k1, back_n2, total_len)
    turned = jnp.stack(
        [back_real * tb_cos - back_imag * tb_sin, back_imag * tb_cos + back_real * tb_sin]
    )
    returned = lax.all_to_all(turned, ("row", "col"), split_axis=4, concat_axis=3, tiled=True)
    cos_last, sin_last = cos_sin(k1_all, n1_all, first_len)
    result = jnp.einsum("gckm,kn->gcnm", returned[0], cos_last, precision=exact_prec)
    result = result - jnp.einsum("gckm,kn->gcnm", returned[1], sin_last, precision=exact_prec)
    result = result * (1.0 / total_len)
    final = lax.all_to_all(result, "row", split_axis=2, concat_axis=3, tiled=True)
    return (final[0], final[1])


def solution(mesh):
    return jax.shard_map(
        local,
        mesh=mesh,
        in_specs=(
            P(None, "row", "col"),
            P(None, None, ("row", "col"), None),
            P(None, None, ("row", "col"), None),
        ),
        out_specs=(P(None, "row", "col"), P(None, "row", "col")),
        check_vma=False,
    )
```

profile of v0, /device:TPU:1, one launch (start us, length us, event | category | flops | bytes accessed | tf_op | source)
XLA Modules:
  0.0 1121.0 jit_solution(2271317239784821227)
XLA Ops:
  12.9 9.4 all-to-all-done
  30.3 10.8 fusion.59
  41.2 10.7 fusion.61
  52.6 13.6 %copy.44 = f32[2,16,1024,16]{3,1,0,2:T(8,128)} copy(f32[2,16,1024,16]{2,3,1,0:T(8,128)S(1)} %pad_maximum_fusion.1) | data formatting | bytes 4194304 | tf_op jit(solution)/shard_map/stack | solution.py:52
  66.2 12.6 %reshape.257 = f32[128,1,4096]{2,1,0:T(1,128)} reshape(f32[1024,2,16,16]{3,2,1,0:T(8,128)} %bitcast.199) | data formatting | bytes 4194304
  78.7 8.3 all-to-all-start.1
  88.0 64.1 %fusion.215 = f32[2048,2048,1]{1,0,2:T(8,128)} fusion(s32[2048]{0:T(1024)S(1)} %fusion.118), kind=kLoop, calls=%fused_computation.23.clone.clone.clone.clone.clone.1 | loop fusion | flops 58720256 | bytes 16785408 | tf_op jit(solution)/shard_map/...n,nq->...q/dot_general | solution.py:25
  159.4 8.9 reshape.258
  168.4 9.4 copy.81
  177.8 16.2 %fusion.181 = (f32[1,16,8,128,16]{4,2,3,1,0:T(8,128)}, f32[1,16,8,128,16]{4,2,3,1,0:T(8,128)}) fusion(f32[2,16,8,128,16]{4,2,3,1,0:T(8,128)S(1)} %bitcast.200), kind=kLoop, calls=%fused_computation.194 | loop fusion | bytes 4194304 | tf_op jit(solution)/shard_map/slice | solution.py:59
  193.9 8.1 copy.46
  202.0 7.9 squeeze.32
  209.9 72.9 %fusion.15 = f32[16,8,2048]{2,1,0:T(8,128)} fusion(f32[16,8,2048]{2,1,0:T(8,128)S(1)} %squeeze.32, s32[2048]{0:T(1024)S(1)} %fusion.118), kind=kOutput, calls=%fused_computation.18 | convolution fusion | flops 6501171200 | bytes 2105344 | tf_op jit(solution)/shard_map/...n,nq->...q/dot_general | solution.py:25
  282.8 8.1 copy.47
  290.8 8.2 squeeze.33
  300.1 71.9 %fusion.17 = f32[16,8,2048]{2,1,0:T(8,128)S(1)} fusion(f32[16,8,2048]{2,1,0:T(8,128)S(1)} %squeeze.33, s32[2048]{0:T(1024)S(1)} %fusion.118), kind=kOutput, calls=%fused_computation.20 | convolution fusion | flops 6501171200 | bytes 2105344 | tf_op jit(solution)/shard_map/...n,nq->...q/dot_general | solution.py:25
  372.0 72.7 %fusion.44 = f32[16,8,2048]{2,1,0:T(8,128)} fusion(f32[16,8,2048]{2,1,0:T(8,128)S(1)} %fusion.17, f32[16,8,2048]{2,1,0:T(8,128)S(1)} %squeeze.32, s32[2048]{0:T(1024)S(1)} %fusion.118), kind=kOutput, calls=%fused_computation.43 | convolution fusion | flops 6501433344 | bytes 3153920 | tf_op jit(solution)/shard_map/...n,nq->...q/dot_general | solution.py:25
  444.7 13.3 %fusion.90 = (f32[1,16,8,2048]{3,2,1,0:T(8,128)}, f32[1,16,8,2048]{3,2,1,0:T(8,128)S(1)}, f32[1,16,8,2048]{3,2,1,0:T(8,128)S(1)}, f32[1,16,8,2048]{3,2,1,0:T(8,128)}) fusion(f32[16,8,2048]{2,1,0:T(8,128)} %fusion.44, f32[2,16,8,2048]{3,2,1,0:T(8,128)} %param.5, f32[2,16,8,2048]{3,2,1,0:T(8,128)} %param.4, f32[16,8,2048]{2,1,0:T(8,128)} %fusion.15, ...), kind=kOutput, calls=%fused_computation.84 | convolution fusion | flops 6445858816 | bytes 28311552 | tf_op jit(solution)/shard_map/...n,nq->...q/dot_general | solution.py:25
  460.7 77.0 %fusion.7 = f32[2,16,8,2048]{3,2,1,0:T(8,128)S(1)} fusion(s32[2048]{0:T(1024)S(1)} %fusion.118, f32[2,16,8,2048]{3,2,1,0:T(8,128)S(1)} %pad_maximum_fusion.19), kind=kOutput, calls=%fused_computation.10 | convolution fusion | flops 12943622144 | bytes 4202496 | tf_op jit(solution)/shard_map/...q,nq->...n/dot_general | solution.py:29
  537.7 77.2 %fusion.9 = f32[2,16,8,2048]{3,2,1,0:T(8,128)S(1)} fusion(s32[2048]{0:T(1024)S(1)} %fusion.118, f32[2,16,8,2048]{3,2,1,0:T(8,128)S(1)} %pad_maximum_fusion.20), kind=kOutput, calls=%fused_computation.12 | convolution fusion | flops 12943622144 | bytes 4202496 | tf_op jit(solution)/shard_map/...q,nq->...n/dot_general | solution.py:29
  614.9 76.5 %fusion.38 = f32[2,16,8,2048]{3,2,1,0:T(8,128)S(1)} fusion(f32[2,16,8,2048]{3,2,1,0:T(8,128)S(1)} %fusion.9, s32[2048]{0:T(1024)S(1)} %fusion.118, f32[2,16,8,2048]{3,2,1,0:T(8,128)S(1)} %pad_maximum_fusion.21), kind=kOutput, calls=%fused_computation.41 | convolution fusion | flops 12944146432 | bytes 6299648 | tf_op jit(solution)/shard_map/...q,nq->...n/dot_general | solution.py:29
  691.5 76.9 %subtract_bitcast_fusion = (f32[1,2,16,8,2048]{4,3,2,1,0:T(8,128)S(1)}, f32[1,2,16,8,2048]{4,3,2,1,0:T(8,128)S(1)}) fusion(f32[2,16,8,2048]{3,2,1,0:T(8,128)S(1)} %fusion.38, f32[8,2048]{1,0:T(8,128)S(1)} %copy-done.4, f32[8,2048]{1,0:T(8,128)S(1)} %copy-done.3, f32[2,16,8,2048]{3,2,1,0:T(8,128)S(1)} %fusion.7, s32[2048]{0:T(1024)S(1)} %fusion.118, ...), kind=kOutput, calls=%fused_computation.58 | convolution fusion | flops 12947292160 | bytes 10625024 | tf_op jit(solution)/shard_map/...q,nq->...n/dot_general | solution.py:29
  770.7 26.4 %copy.48 = f32[2,2,16,8,2048]{2,3,1,0,4:T(8,128)} copy(f32[2,2,16,8,2048]{4,3,2,1,0:T(8,128)} %pad_maximum_fusion) | data formatting | bytes 8388608 | tf_op jit(solution)/shard_map/stack | solution.py:74
  797.1 23.5 %reshape.259 = f32[128,1,8192]{2,1,0:T(1,128)} reshape(f32[2048,2,2,8,16]{4,3,2,1,0:T(8,128)} %bitcast.194) | data formatting | bytes 8388608
  820.6 61.6 %all_to_all.63 = f32[128,1,8192]{2,1,0:T(1,128)} all-to-all(f32[128,1,8192]{2,1,0:T(1,128)} %reshape.259), channel_id=1, replica_groups=mesh['row'=16,'col'=8] {'row','col'}, dimensions={0} | all-to-all | bytes 8388608 | tf_op jit(solution)/shard_map/all_to_all | solution.py:77
  882.2 13.9 %reduce.2 = f32[128,8192]{1,0:T(8,128)} reduce(f32[128,1,8192]{2,1,0:T(1,128)} %all_to_all.63, f32[]{:T(128)} %broadcast.476), dimensions={1}, to_apply=%all_to_all.53.reduce_sub_computation | reduce | bytes 8388612 | tf_op jit(solution)/shard_map/all_to_all | solution.py:77
  896.1 18.9 %reshape.260 = f32[2048,2,2,8,16]{4,3,2,1,0:T(8,128)} reshape(f32[128,8192]{1,0:T(8,128)} %reduce.2) | data formatting | bytes 8388608
  915.0 40.6 %copy.65 = f32[2,2,16,8,128,16]{5,4,3,2,1,0:T(8,128)} copy(f32[2,2,16,8,128,16]{2,3,1,0,5,4:T(8,128)} %bitcast.196) | data formatting | bytes 8388608 | tf_op jit(solution)/shard_map/all_to_all | solution.py:77
  955.6 17.7 %fusion.180 = (f32[1,2,16,128,8,16]{5,3,4,2,1,0:T(8,128)S(1)}, f32[1,2,16,128,8,16]{5,3,4,2,1,0:T(8,128)}) fusion(f32[2,2,16,128,8,16]{5,3,4,2,1,0:T(8,128)} %bitcast.195), kind=kLoop, calls=%fused_computation.193 | loop fusion | bytes 8388608 | tf_op jit(solution)/shard_map/slice | solution.py:79
  973.3 47.8 %fusion.3 = f32[512,2,16,16]{0,3,2,1:T(8,128)S(1)} fusion(f32[1,2,16,128,8,16]{5,3,4,2,1,0:T(8,128)} %get-tuple-element.9), kind=kOutput, calls=%fused_computation.6 | convolution fusion | flops 3228565504 | bytes 3145728 | tf_op jit(solution)/shard_map/gckm,kn->gcnm/dot_general | solution.py:80
  1021.1 41.6 %fusion.80 = f32[2,16,512,16]{2,3,1,0:T(8,128)S(1)} fusion(f32[512,2,16,16]{0,3,2,1:T(8,128)S(1)} %fusion.3, f32[1,2,16,128,8,16]{5,3,4,2,1,0:T(8,128)S(1)} %get-tuple-element.8), kind=kOutput, calls=%fused_computation.72 | convolution fusion | flops 3229089792 | bytes 4194304 | tf_op jit(solution)/shard_map/gckm,kn->gcnm/dot_general | solution.py:79
  1076.5 20.9 %all_to_all.64 = f32[16,1,16384]{2,1,0:T(1,128)S(1)} all-to-all(f32[16,1,16384]{2,1,0:T(1,128)S(1)} %reshape.261), channel_id=1, replica_groups=mesh['row'=16,'col'=8] {'row'}, dimensions={0} | all-to-all | bytes 2097152 | tf_op jit(solution)/shard_map/all_to_all | solution.py:82
  (49 shorter events, 72.1 us)
Async XLA Ops:
  4.7 17.6 %all-to-all-start = ((f32[16,1,8192]{2,1,0:T(1,128)}), f32[16,1,8192]{2,1,0:T(1,128)S(1)}, u32[]{:S(2)}, u32[]{:S(2)}) async-start(f32[16,1,8192]{2,1,0:T(1,128)} %reshape.255), calls=%async_computation | async-start | bytes 1048576 | tf_op jit(solution)/shard_map/all_to_all | solution.py:44
  78.7 73.4 %all-to-all-start.1 = ((f32[128,1,4096]{2,1,0:T(1,128)}), f32[128,1,4096]{2,1,0:T(1,128)}, u32[]{:S(2)}, u32[]{:S(2)}) async-start(f32[128,1,4096]{2,1,0:T(1,128)} %reshape.257), calls=%async_computation.1 | async-start | bytes 4194304 | tf_op jit(solution)/shard_map/all_to_all | solution.py:56
  299.1 1.0 copy-start.2
  300.1 144.6 %slice-start = ((s8[16777216]{0:T(1024)(128)(4,1)}), s8[4194304]{0:T(1024)(128)(4,1)S(1)}, s32[]{:S(2)}) async-start(s8[16777216]{0:T(1024)(128)(4,1)} %bitcast.197), calls=%async_computation.4 | async-start | bytes 8388608
  300.1 144.6 %slice-start.1 = ((s8[16777216]{0:T(1024)(128)(4,1)}), s8[4194304]{0:T(1024)(128)(4,1)S(1)}, s32[]{:S(2)}) async-start(s8[16777216]{0:T(1024)(128)(4,1)} %bitcast.197), calls=%async_computation.5 | async-start | bytes 8388608
  372.0 72.7 %slice-start.2 = ((s8[16777216]{0:T(1024)(128)(4,1)}), s8[4194304]{0:T(1024)(128)(4,1)S(1)}, s32[]{:S(2)}) async-start(s8[16777216]{0:T(1024)(128)(4,1)} %bitcast.197), calls=%async_computation.6 | async-start | bytes 8388608
  372.0 72.7 %slice-start.3 = ((s8[16777216]{0:T(1024)(128)(4,1)}), s8[4194304]{0:T(1024)(128)(4,1)S(1)}, s32[]{:S(2)}) async-start(s8[16777216]{0:T(1024)(128)(4,1)} %bitcast.197), calls=%async_computation.7 | async-start | bytes 8388608
  458.0 1.9 copy-start
  458.1 2.2 copy-start.1
  614.9 76.6 %copy-start.3 = (f32[8,2048]{1,0:T(8,128)S(1)}, f32[8,2048]{1,0:T(8,128)}, u32[]{:S(2)}) copy-start(f32[8,2048]{1,0:T(8,128)} %get-tuple-element.24) | copy-start | bytes 196612
  614.9 76.6 %copy-start.4 = (f32[8,2048]{1,0:T(8,128)S(1)}, f32[8,2048]{1,0:T(8,128)}, u32[]{:S(2)}) copy-start(f32[8,2048]{1,0:T(8,128)} %get-tuple-element.25) | copy-start | bytes 196612
where the time goes:
time: 1130 us; the launch traced here: 1120 us
  matrix products  649 us (57%)
  local copies, waits for them, and re-layouts  265 us (23%)
  other arithmetic  97 us (9%)
  blocking collectives  82.5 us (7%)
  starting transfers between devices  16.1 us (1%)
    dot_general x4, matrix products, backward_table(): return jnp.einsum('...q,nq->...n', values, table, precision=exact_prec)  308 us
    dot_general x4, matrix products, forward_table(): return jnp.einsum('...n,nq->...q', values, table, precision=exact_prec)  231 us
    unnamed x29, local copies, waits for them, and re-layouts  85.4 us
    dot_general x1, other arithmetic, forward_table(): return jnp.einsum('...n,nq->...q', values, table, precision=exact_prec)  64.1 us
    all_to_all x1, blocking collectives, local(): lax.all_to_all(turned, ('row', 'col'), split_axis=4, concat_axis=3, tiled...  61.6 us
    dot_general x1, matrix products, local(): jnp.einsum('gckm,kn->gcnm', returned[1], sin_last, precision=exact_prec)  47.8 us
    dot_general x1, matrix products, local(): jnp.einsum('gckm,kn->gcnm', returned[0], cos_last, precision=exact_prec)  41.6 us
    all_to_all x1, local copies, waits for them, and re-layouts, local(): lax.all_to_all(turned, ('row', 'col'), split_axis=4, concat_axis=3, tiled...  40.6 us
  transfers between devices with their start and end apart: 2, of which 1 were waited for; matrix products, arithmetic and copies ran while one was open for 6% of the time, Pallas kernels for 0%

commit v1 on v0

v1 whole, which is shorter than its diff:
```python
import functools

import jax
import jax.numpy as jnp
import ml_dtypes
import numpy as np
from jax import lax
from jax.experimental import pallas as pl
from jax.experimental.pallas import tpu as pltpu
from jax.sharding import PartitionSpec as P

MESH = pl.DeviceIdType.MESH
F32 = jnp.float32
BF16 = jnp.bfloat16

ROWS, COLS = 16, 8
DEVS = ROWS * COLS
CH = 16
N1, N2 = 1024, 2048
HALF1 = N1 // 2
TOTAL = N1 * N2
K1L = N1 // DEVS
N1L = HALF1 // ROWS
B = N2 // COLS
RAD = 8
GROUPS, PER = 4, 4
ROOT_HALF = float(np.sqrt(0.5))


def split_table(table):
    table = np.asarray(table, np.float64)
    high = table.astype(np.float32).astype(ml_dtypes.bfloat16)
    low = (table - high.astype(np.float64)).astype(np.float32).astype(ml_dtypes.bfloat16)
    return np.stack([high, low])


@functools.lru_cache(None)
def tables():
    n1 = np.arange(HALF1)
    k1 = np.arange(N1)
    angle = 2 * np.pi * ((k1[:, None] * n1[None, :]) % N1) / N1
    first = np.stack([np.cos(angle), -np.sin(angle)]).reshape(2, DEVS, K1L, HALF1)
    first = first.transpose(1, 0, 2, 3).reshape(2 * N1, HALF1)
    last = (first.T / TOTAL).reshape(HALF1, ROWS, 2 * N1 // ROWS).transpose(1, 0, 2)
    b = np.arange(B)
    angle = 2 * np.pi * ((b[:, None] * b[None, :]) % B) / B
    c, s = np.cos(angle), np.sin(angle)
    inner = np.block([[c, -s], [s, c]])
    back = np.block([[c, s], [-s, c]])
    place = np.zeros((B, B))
    place[b, (b % RAD) * (B // RAD) + b // RAD] = 1
    return (
        split_table(first),
        split_table(last),
        np.concatenate([split_table(inner), split_table(back)]),
        place.astype(ml_dtypes.bfloat16),
    )


def split(value):
    high = value.astype(BF16)
    low = (value - high.astype(F32)).astype(BF16)
    return high, low


def mm(a, b):
    return jnp.dot(a, b, preferred_element_type=F32)


def mm3(ah, al, bh, bl):
    return mm(ah, bh) + (mm(ah, bl) + mm(al, bh))


def dft4(re, im, sign):
    p0r, p0i = re[0] + re[2], im[0] + im[2]
    p1r, p1i = re[0] - re[2], im[0] - im[2]
    r0r, r0i = re[1] + re[3], im[1] + im[3]
    r1r, r1i = re[1] - re[3], im[1] - im[3]
    out_r = [p0r + r0r, None, p0r - r0r, None]
    out_i = [p0i + r0i, None, p0i - r0i, None]
    if sign > 0:
        out_r[1], out_i[1] = p1r - r1i, p1i + r1r
        out_r[3], out_i[3] = p1r + r1i, p1i - r1r
    else:
        out_r[1], out_i[1] = p1r + r1i, p1i - r1r
        out_r[3], out_i[3] = p1r - r1i, p1i + r1r
    return out_r, out_i


def dft8(re, im, sign):
    ur = [re[a] + re[a + 4] for a in range(4)]
    ui = [im[a] + im[a + 4] for a in range(4)]
    vr = [re[a] - re[a + 4] for a in range(4)]
    vi = [im[a] - im[a + 4] for a in range(4)]
    even_r, even_i = dft4(ur, ui, sign)
    if sign > 0:
        v1 = ((vr[1] - vi[1]) * ROOT_HALF, (vi[1] + vr[1]) * ROOT_HALF)
        v2 = (-vi[2], vr[2])
        v3 = ((vr[3] + vi[3]) * -ROOT_HALF, (vr[3] - vi[3]) * ROOT_HALF)
    else:
        v1 = ((vr[1] + vi[1]) * ROOT_HALF, (vi[1] - vr[1]) * ROOT_HALF)
        v2 = (vi[2], -vr[2])
        v3 = ((vi[3] - vr[3]) * ROOT_HALF, (vr[3] + vi[3]) * -ROOT_HALF)
    odd_r, odd_i = dft4([vr[0], v1[0], v2[0], v3[0]], [vi[0], v1[1], v2[1], v3[1]], sign)
    out_r = [None] * 8
    out_i = [None] * 8
    for t in range(4):
        out_r[2 * t], out_i[2 * t] = even_r[t], even_i[t]
        out_r[2 * t + 1], out_i[2 * t + 1] = odd_r[t], odd_i[t]
    return out_r, out_i


def row_at(row, q, m, way):
    yl, z, core = lax.div(row, 8), lax.rem(lax.div(row, 2), 4), lax.rem(row, 2)
    dyl, dc, dz = lax.div(m, 2), lax.rem(m, 2), lax.rem(q + m, 4)
    dz = dz if way > 0 else 4 - dz
    return lax.rem(yl + dyl, 2) * 8 + lax.rem(z + dz, 4) * 2 + lax.rem(core + dc, 2)


def col_at(col, i):
    yh, x = lax.div(col, 4), lax.rem(col, 4)
    return lax.rem(yh + lax.div(i, 4), 2) * 4 + lax.rem(x + lax.rem(i, 4), 4)


def loop(lower, upper, body):
    def step(i, carry):
        body(i)
        return carry

    lax.fori_loop(lower, upper, step, 0)


def kernel(
    grad_ref, sx_ref, sh_ref, first_ref, last_ref, inner_ref, place_ref,
    oh_ref, ox_ref,
    raw, spec, first, last, inner, place, xg, xs, bsend, brecv, va, vt,
    ah, al, us, vs, tsend, trecv, acc,
    lsem, s1, r1, s2, r2, s4, r4, s5, r5,
):
    row = lax.axis_index("row")
    col = lax.axis_index("col")
    me = row * COLS + col

    barrier = pltpu.get_barrier_semaphore()

    def greet(i):
        d = lax.rem(me + i, DEVS)
        pl.semaphore_signal(
            barrier, inc=1, device_id=(lax.div(d, COLS), lax.rem(d, COLS)), device_id_type=MESH
        )

    loop(1, DEVS, greet)

    loads = [
        pltpu.make_async_copy(sh_ref, raw.at[0], lsem.at[0]),
        pltpu.make_async_copy(sx_ref, raw.at[1], lsem.at[1]),
        pltpu.make_async_copy(place_ref, place, lsem.at[2]),
        pltpu.make_async_copy(first_ref, first, lsem.at[3]),
        pltpu.make_async_copy(inner_ref, inner, lsem.at[4]),
        pltpu.make_async_copy(last_ref, last, lsem.at[5]),
    ]
    for load in loads:
        load.start()

    k1 = me * K1L + lax.broadcasted_iota(jnp.int32, (K1L, B), 0)
    lane = lax.broadcasted_iota(jnp.int32, (K1L, B), 1)

    def turn(a):
        phase = lax.rem(k1 * a, TOTAL // B)
        phase = jnp.where(phase > TOTAL // B // 2, phase - TOTAL // B, phase)
        angle = phase.astype(F32) * (2.0 * np.pi * B / TOTAL)
        va[0, a] = jnp.cos(angle)
        va[1, a] = jnp.sin(angle)
        phase = lane * (k1 + N1 * a)
        phase = jnp.where(phase > TOTAL // 2, phase - TOTAL, phase)
        angle = phase.astype(F32) * (2.0 * np.pi / TOTAL)
        vt[0, a] = jnp.cos(angle)
        vt[1, a] = jnp.sin(angle)

    loop(0, RAD, turn)

    pl.semaphore_wait(barrier, DEVS - 1)

    own_rows = pl.ds(pl.multiple_of(row * N1L, N1L), N1L)
    own_x = pltpu.make_async_copy(grad_ref.at[row], xg.at[own_rows], r1)
    own_x.start()

    def send_x(i):
        r = lax.rem(row + i, ROWS)
        pltpu.make_async_remote_copy(
            src_ref=grad_ref.at[r], dst_ref=xg.at[own_rows], send_sem=s1, recv_sem=r1,
            device_id=(r, col), device_id_type=MESH,
        ).start()

    loop(1, ROWS, send_x)

    for load in loads[:3]:
        load.wait()
    lane128 = lax.broadcasted_iota(jnp.int32, (16, 128), 1)

    def order(n):
        which, part, c0 = lax.div(n, 8), lax.rem(lax.div(n, 4), 2), lax.rem(n, 4) * 4
        blocks = []
        for c in range(4):
            whole = raw[which, part, c0 + c]
            blocks += [whole[:, j * B : (j + 1) * B] for j in range(RAD)]
        high, low = split(jnp.concatenate(blocks, axis=0))
        placed = mm(high, place[...]) + mm(low, place[...])
        for c in range(4):
            for h in range(2):
                runs = []
                for i in range(4):
                    at = c * 64 + i * 8
                    runs.append(
                        jnp.concatenate(
                            [
                                placed[at : at + 8, h * 128 : h * 128 + 128],
                                placed[at + 32 : at + 40, h * 128 : h * 128 + 128],
                            ],
                            axis=0,
                        )
                    )
                for tt in range(4):
                    t = 4 * h + tt
                    total = None
                    for i in range(4):
                        shift = (32 * (i - tt)) % 128
                        moved = pltpu.roll(runs[i], shift, 1) if shift else runs[i]
                        if total is None:
                            total = moved
                        else:
                            total = jnp.where(lane128 >= 32 * i, moved, total)
                    spec[which, part, c0 + c, t * 8 : t * 8 + 8, 0:128] = total[0:8]
                    spec[which, part, c0 + c, t * 8 : t * 8 + 8, 128:256] = total[8:16]

    loop(0, 16, order)

    loads[3].wait()
    pltpu.make_async_copy(xg, xg, r1).wait()
    high, low = split(xg[...])
    xs[0] = high
    xs[1] = low

    def first_group(q):
        rows = [row_at(row, q, m, 1) for m in range(PER)]
        at = [pl.ds(pl.multiple_of(r * 128, 128), 128) for r in rows]
        wh = jnp.concatenate([first[0, a] for a in at], axis=0)
        wl = jnp.concatenate([first[1, a] for a in at], axis=0)
        value = mm3(wh, wl, xs[0], xs[1])
        for m in range(PER):
            block = value[m * 128 : (m + 1) * 128].reshape(COLS, 2, K1L, B)
            bsend[pl.ds(rows[m] * COLS, COLS)] = block

        @pl.when(q == 0)
        def _():
            pltpu.make_async_copy(bsend.at[me], brecv.at[me], r2.at[q]).start()

        def send(e):
            r = row_at(row, q, lax.rem(e, PER), 1)
            c = col_at(col, lax.div(e, PER))
            pltpu.make_async_remote_copy(
                src_ref=bsend.at[r * COLS + c], dst_ref=brecv.at[me], send_sem=s2,
                recv_sem=r2.at[q], device_id=(r, c), device_id_type=MESH,
            ).start()

        loop(jnp.where(q == 0, 1, 0), PER * COLS, send)

    loop(0, GROUPS, first_group)

    loads[4].wait()

    def inverse(which, q):
        def product(m):
            c = row_at(row, q, m, -1)
            at = pl.ds(pl.multiple_of(m * 64, 64), 64)
            ur, ui = us[q, at, 0:B], us[q, at, B : 2 * B]
            sr, si = spec[which, 0, c], spec[which, 1, c]
            high, low = split(ur * sr + ui * si)
            ah[at, 0:B] = high
            al[at, 0:B] = low
            high, low = split(ui * sr - ur * si)
            ah[at, B : 2 * B] = high
            al[at, B : 2 * B] = low

        loop(0, PER, product)
        vs[...] = mm3(ah[...], al[...], inner[2], inner[3])

        def turn_back(m):
            c = row_at(row, q, m, -1)
            re, im = [], []
            for t in range(RAD):
                at = pl.ds(pl.multiple_of(m * 64 + t * 8, 8), 8)
                r, i = vs[at, 0:B], vs[at, B : 2 * B]
                cs, sn = vt[0, t], vt[1, t]
                re.append(r * cs - i * sn)
                im.append(i * cs + r * sn)
            re, im = dft8(re, im, 1)
            for a in range(RAD):
                r, i = re[a], im[a]
                if a:
                    cs, sn = va[0, a], va[1, a]
                    r, i = r * cs - i * sn, i * cs + r * sn
                tsend[which, c * COLS + a, 0] = r
                tsend[which, c * COLS + a, 1] = i

        loop(0, PER, turn_back)

        @pl.when(q == 0)
        def _():
            pltpu.make_async_copy(tsend.at[which, me], trecv.at[which, me], r4.at[which, q]).start()

        def send(e):
            r = row_at(row, q, lax.rem(e, PER), -1)
            c = col_at(col, lax.div(e, PER))
            pltpu.make_async_remote_copy(
                src_ref=tsend.at[which, r * COLS + c], dst_ref=trecv.at[which, me],
                send_sem=s4.at[which], recv_sem=r4.at[which, q], device_id=(r, c),
                device_id_type=MESH,
            ).start()

        loop(jnp.where(q == 0, 1, 0), PER * COLS, send)

    def forward(q):
        group = brecv.at[pl.ds(0, PER * COLS)]
        pltpu.make_async_copy(group, group, r2.at[q]).wait()

        def outer(m):
            c = row_at(row, q, m, -1)
            re, im = [], []
            for a in range(RAD):
                r, i = brecv[c * COLS + a, 0], brecv[c * COLS + a, 1]
                if a:
                    cs, sn = va[0, a], va[1, a]
                    r, i = r * cs + i * sn, i * cs - r * sn
                re.append(r)
                im.append(i)
            re, im = dft8(re, im, -1)
            out_r, out_i = [], []
            for t in range(RAD):
                cs, sn = vt[0, t], vt[1, t]
                out_r.append(re[t] * cs + im[t] * sn)
                out_i.append(im[t] * cs - re[t] * sn)
            at = pl.ds(pl.multiple_of(m * 64, 64), 64)
            high, low = split(jnp.concatenate(out_r, axis=0))
            ah[at, 0:B] = high
            al[at, 0:B] = low
            high, low = split(jnp.concatenate(out_i, axis=0))
            ah[at, B : 2 * B] = high
            al[at, B : 2 * B] = low

        loop(0, PER, outer)
        us[q] = mm3(ah[...], al[...], inner[0], inner[1])
        inverse(0, q)

    loop(0, GROUPS, forward)
    loop(0, GROUPS, lambda q: inverse(1, q))

    loads[5].wait()

    for which, out in ((0, oh_ref), (1, ox_ref)):

        def last_group(q):
            group = trecv.at[which, pl.ds(0, PER * COLS)]
            pltpu.make_async_copy(group, group, r4.at[which, q]).wait()
            rows = [row_at(row, q, m, 1) for m in range(PER)]
            high, low = split(
                jnp.concatenate(
                    [trecv[which, pl.ds(r * COLS, COLS)].reshape(128, B) for r in rows], axis=0
                )
            )
            wh = jnp.concatenate([last[0, r] for r in rows], axis=1)
            wl = jnp.concatenate([last[1, r] for r in rows], axis=1)
            value = mm3(wh, wl, high, low)

            @pl.when(q == 0)
            def _():
                acc[which] = value

            @pl.when(q > 0)
            def _():
                acc[which] += value

        loop(0, GROUPS, last_group)
        pltpu.make_async_copy(acc.at[which, own_rows], out.at[row], r5.at[which]).start()

        def send_out(i):
            r = lax.rem(row + i, ROWS)
            pltpu.make_async_remote_copy(
                src_ref=acc.at[which, pl.ds(pl.multiple_of(r * N1L, N1L), N1L)],
                dst_ref=out.at[row], send_sem=s5.at[which], recv_sem=r5.at[which],
                device_id=(r, col), device_id_type=MESH,
            ).start()

        loop(1, ROWS, send_out)

    other_rows = xg.at[pl.ds(0, (ROWS - 1) * N1L)]
    pltpu.make_async_copy(other_rows, other_rows, s1).wait()
    others = bsend.at[pl.ds(0, DEVS - 1)]
    pltpu.make_async_copy(others, others, s2).wait()
    for which, out in ((0, oh_ref), (1, ox_ref)):
        others = tsend.at[which, pl.ds(0, DEVS - 1)]
        pltpu.make_async_copy(others, others, s4.at[which]).wait()
        other_rows = acc.at[which, pl.ds(0, (ROWS - 1) * N1L)]
        pltpu.make_async_copy(other_rows, other_rows, s5.at[which]).wait()
        pltpu.make_async_copy(out, out, r5.at[which]).wait()


def local(grad_out, input_spectrum, filter_spectrum):
    first, last, inner, place = (jnp.asarray(t) for t in tables())
    out = jax.ShapeDtypeStruct((CH, N1L, B), F32)
    dma = pltpu.SemaphoreType.DMA
    return pl.pallas_call(
        kernel,
        out_shape=(out, out),
        in_specs=[pl.BlockSpec(memory_space=pl.ANY)] * 7,
        out_specs=(pl.BlockSpec(memory_space=pl.ANY),) * 2,
        scratch_shapes=[
            pltpu.VMEM((2, 2, CH, K1L, N2), F32),
            pltpu.VMEM((2, 2, CH, RAD * K1L, B), F32),
            pltpu.VMEM((2, 2 * N1, HALF1), BF16),
            pltpu.VMEM((2, ROWS, HALF1, 128), BF16),
            pltpu.VMEM((4, 2 * B, 2 * B), BF16),
            pltpu.VMEM((B, B), BF16),
            pltpu.VMEM((HALF1, B), F32),
            pltpu.VMEM((2, HALF1, B), BF16),
            pltpu.VMEM((DEVS, 2, K1L, B), F32),
            pltpu.VMEM((DEVS, 2, K1L, B), F32),
            pltpu.VMEM((2, RAD, K1L, B), F32),
            pltpu.VMEM((2, RAD, K1L, B), F32),
            pltpu.VMEM((PER * 64, 2 * B), BF16),
            pltpu.VMEM((PER * 64, 2 * B), BF16),
            pltpu.VMEM((GROUPS, PER * 64, 2 * B), F32),
            pltpu.VMEM((PER * 64, 2 * B), F32),
            pltpu.VMEM((2, DEVS, 2, K1L, B), F32),
            pltpu.VMEM((2, DEVS, 2, K1L, B), F32),
            pltpu.VMEM((2, HALF1, B), F32),
            dma((6,)),
            dma, dma,
            dma, dma((GROUPS,)),
            dma((2,)), dma((2, GROUPS)),
            dma((2,)), dma((2,)),
        ],
        compiler_params=pltpu.CompilerParams(
            collective_id=0, has_side_effects=True, vmem_limit_bytes=56 * 2**20
        ),
    )(grad_out, input_spectrum, filter_spectrum, first, last, inner, place)


def solution(mesh):
    return jax.shard_map(
        local,
        mesh=mesh,
        in_specs=(
            P(None, "row", "col"),
            P(None, None, ("row", "col"), None),
            P(None, None, ("row", "col"), None),
        ),
        out_specs=(P(None, "row", "col"), P(None, "row", "col")),
        check_vma=False,
    )
```

time: 1130 us -> 118 us (0.10)
  matrix products: 649 us -> 0 us
  local copies, waits for them, and re-layouts: 265 us -> 3.76 us
  Pallas kernels: 0 us -> 114 us
  other arithmetic: 97 us -> 0 us
  blocking collectives: 82.5 us -> 0 us
  starting transfers between devices: 16.1 us -> 0 us
    dot_general x10 -> x0, matrix products: 628 us -> none  [the longest x4 308 us: backward_table(): return jnp.einsum('...q,nq->...n', values, table, precision=exact_prec)]
    pallas_call x0 -> x1, Pallas kernels: none -> 114 us  [local(): pl.pallas_call(kernel, out_shape=(out, out), in_specs=[pl.BlockSpec(memor...]
    all_to_all x2 -> x0, blocking collectives: 82.5 us -> none  [the longest x1 61.6 us: local(): lax.all_to_all(turned, ('row', 'col'), split_axis=4, concat_axis=3, tiled...]
    unnamed x29 -> x2, local copies, waits for them, and re-layouts: 85.4 us -> 3.76 us
    dot_general x5 -> x0, other arithmetic: 66.4 us -> none  [the longest x1 64.1 us: forward_table(): return jnp.einsum('...n,nq->...q', values, table, precision=exact_prec)]
    all_to_all x6 -> x0, local copies, waits for them, and re-layouts: 62.3 us -> none  [the longest x1 40.6 us: local(): lax.all_to_all(turned, ('row', 'col'), split_axis=4, concat_axis=3, tiled...]
    slice x5 -> x0, local copies, waits for them, and re-layouts: 54 us -> none  [the longest x2 24.2 us: local(): moved[0]]
    another operation x2 -> x0, local copies, waits for them, and re-layouts: 40 us -> none  [the longest x1 26.4 us: local(): jnp.stack([back_real * tb_cos - back_imag * tb_sin, back_imag * tb_cos +...]
  transfers between devices with their start and end apart: 2 -> 0, of which waited for: 1 -> 0; matrix products, arithmetic and copies ran while one was open for 6% -> 0% of each run, Pallas kernels for 0% -> 0%
where the time goes in v1:
time: 118 us
  Pallas kernels  114 us (97%)
  local copies, waits for them, and re-layouts  3.76 us (3%)
    pallas_call x1, Pallas kernels, local(): pl.pallas_call(kernel, out_shape=(out, out), in_specs=[pl.BlockSpec(memor...  114 us
    unnamed x2, local copies, waits for them, and re-layouts  3.76 us

profile of v1, /device:TPU:1, one launch (start us, length us, event | category | flops | bytes accessed | tf_op | source)
XLA Modules:
  0.0 118.3 jit_solution(7788439261536255374)
XLA Ops:
  0.6 113.9 %shard_map.86 = (f32[16,32,256]{2,1,0:T(8,128)}, f32[16,32,256]{2,1,0:T(8,128)}) custom-call(f32[16,32,256]{2,1,0:T(8,128)} %grad_ref.1, f32[2,16,8,2048]{3,2,1,0:T(8,128)} %sx_ref.1, f32[2,16,8,2048]{3,2,1,0:T(8,128)} %sh_ref.1, bf16[2,2048,512]{2,1,0:T(8,128)(2,1)} %constant.8.clone.first_ref, bf16[2,16,512,128]{3,2,1,0:T(8,128)(2,1)} %constant.9.clone.last_ref, ...), custom_call_target="tpu_custom_call" | custom-call | tf_op jit(solution)/shard_map/pallas_call | solution.py:412
  114.5 1.9 %copy.11 = f32[16,32,256]{2,1,0:T(8,128)} copy(f32[16,32,256]{2,1,0:T(8,128)} %get-tuple-element.4) | data formatting | bytes 1048576
  116.4 1.9 %copy.12 = f32[16,32,256]{2,1,0:T(8,128)} copy(f32[16,32,256]{2,1,0:T(8,128)} %get-tuple-element.5) | data formatting | bytes 1048576

commit v2 on v1

--- a/solution.py
+++ b/solution.py
@@ -24,6 +24,7 @@
 B = N2 // COLS
 RAD = 8
 GROUPS, PER = 4, 4
+UNITS = ((0, pl.ds(0, B)), (1, pl.ds(0, B // 2)), (1, pl.ds(B // 2, B // 2)))
 ROOT_HALF = float(np.sqrt(0.5))
 
 
@@ -130,6 +131,18 @@
     lax.fori_loop(lower, upper, step, 0)
 
 
+def spread(row, col, q, way, send):
+    least = jnp.where(q == 0, 1, 0)
+    count = PER * COLS - least
+    start = (row * COLS + col) * 29
+
+    def step(i):
+        e = least + lax.rem(i * 13 + start, count)
+        send(row_at(row, q, lax.rem(e, PER), way), col_at(col, lax.div(e, PER)))
+
+    loop(0, count, step)
+
+
 def kernel(
     grad_ref, sx_ref, sh_ref, first_ref, last_ref, inner_ref, place_ref,
     oh_ref, ox_ref,
@@ -144,12 +157,18 @@
     barrier = pltpu.get_barrier_semaphore()
 
     def greet(i):
-        d = lax.rem(me + i, DEVS)
-        pl.semaphore_signal(
-            barrier, inc=1, device_id=(lax.div(d, COLS), lax.rem(d, COLS)), device_id_type=MESH
-        )
-
-    loop(1, DEVS, greet)
+        r = row + i
+        r = jnp.where(r >= ROWS, r - ROWS, r)
+        for j in range(COLS):
+            c = col + j
+            c = jnp.where(c >= COLS, c - COLS, c)
+            pl.semaphore_signal(barrier, inc=1, device_id=(r, c), device_id_type=MESH)
+
+    for j in range(1, COLS):
+        c = col + j
+        c = jnp.where(c >= COLS, c - COLS, c)
+        pl.semaphore_signal(barrier, inc=1, device_id=(row, c), device_id_type=MESH)
+    loop(1, ROWS, greet)
 
     loads = [
         pltpu.make_async_copy(sh_ref, raw.at[0], lsem.at[0]),
@@ -255,19 +274,36 @@
         def _():
             pltpu.make_async_copy(bsend.at[me], brecv.at[me], r2.at[q]).start()
 
-        def send(e):
-            r = row_at(row, q, lax.rem(e, PER), 1)
-            c = col_at(col, lax.div(e, PER))
+        def send(r, c):
             pltpu.make_async_remote_copy(
                 src_ref=bsend.at[r * COLS + c], dst_ref=brecv.at[me], send_sem=s2,
                 recv_sem=r2.at[q], device_id=(r, c), device_id_type=MESH,
             ).start()
 
-        loop(jnp.where(q == 0, 1, 0), PER * COLS, send)
+        spread(row, col, q, 1, send)
 
     loop(0, GROUPS, first_group)
 
     loads[4].wait()
+
+    def send_back(unit, q):
+        which, lanes = UNITS[unit]
+
+        @pl.when(q == 0)
+        def _():
+            pltpu.make_async_copy(
+                tsend.at[which, me, :, :, lanes], trecv.at[which, me, :, :, lanes], r4.at[unit, q]
+            ).start()
+
+        def send(r, c):
+            pltpu.make_async_remote_copy(
+                src_ref=tsend.at[which, r * COLS + c, :, :, lanes],
+                dst_ref=trecv.at[which, me, :, :, lanes],
+                send_sem=s4.at[unit], recv_sem=r4.at[unit, q], device_id=(r, c),
+                device_id_type=MESH,
+            ).start()
+
+        spread(row, col, q, -1, send)
 
     def inverse(which, q):
         def product(m):
@@ -305,20 +341,6 @@
 
         loop(0, PER, turn_back)
 
-        @pl.when(q == 0)
-        def _():
-            pltpu.make_async_copy(tsend.at[which, me], trecv.at[which, me], r4.at[which, q]).start()
-
-        def send(e):
-            r = row_at(row, q, lax.rem(e, PER), -1)
-            c = col_at(col, lax.div(e, PER))
-            pltpu.make_async_remote_copy(
-                src_ref=tsend.at[which, r * COLS + c], dst_ref=trecv.at[which, me],
-                send_sem=s4.at[which], recv_sem=r4.at[which, q], device_id=(r, c),
-                device_id_type=MESH,
-            ).start()
-
-        loop(jnp.where(q == 0, 1, 0), PER * COLS, send)
 
     def forward(q):
         group = brecv.at[pl.ds(0, PER * COLS)]
@@ -351,43 +373,49 @@
         loop(0, PER, outer)
         us[q] = mm3(ah[...], al[...], inner[0], inner[1])
         inverse(0, q)
+        send_back(0, q)
+
+    def second(q):
+        inverse(1, q)
+        send_back(1, q)
 
     loop(0, GROUPS, forward)
-    loop(0, GROUPS, lambda q: inverse(1, q))
+    loop(0, GROUPS, second)
+    loop(0, GROUPS, lambda q: send_back(2, q))
 
     loads[5].wait()
 
-    for which, out in ((0, oh_ref), (1, ox_ref)):
+    for unit, (which, lanes) in enumerate(UNITS):
+        out = (oh_ref, ox_ref)[which]
 
         def last_group(q):
-            group = trecv.at[which, pl.ds(0, PER * COLS)]
-            pltpu.make_async_copy(group, group, r4.at[which, q]).wait()
+            group = trecv.at[which, pl.ds(0, PER * COLS), :, :, lanes]
+            pltpu.make_async_copy(group, group, r4.at[unit, q]).wait()
             rows = [row_at(row, q, m, 1) for m in range(PER)]
-            high, low = split(
-                jnp.concatenate(
-                    [trecv[which, pl.ds(r * COLS, COLS)].reshape(128, B) for r in rows], axis=0
-                )
-            )
+            parts = [trecv[which, pl.ds(r * COLS, COLS), :, :, lanes] for r in rows]
+            high, low = split(jnp.concatenate([p.reshape(128, p.shape[-1]) for p in parts], axis=0))
             wh = jnp.concatenate([last[0, r] for r in rows], axis=1)
             wl = jnp.concatenate([last[1, r] for r in rows], axis=1)
             value = mm3(wh, wl, high, low)
 
             @pl.when(q == 0)
             def _():
-                acc[which] = value
+                acc[which, :, lanes] = value
 
             @pl.when(q > 0)
             def _():
-                acc[which] += value
+                acc[which, :, lanes] += value
 
         loop(0, GROUPS, last_group)
-        pltpu.make_async_copy(acc.at[which, own_rows], out.at[row], r5.at[which]).start()
+        pltpu.make_async_copy(
+            acc.at[which, own_rows, lanes], out.at[row, :, lanes], r5.at[unit]
+        ).start()
 
         def send_out(i):
             r = lax.rem(row + i, ROWS)
             pltpu.make_async_remote_copy(
-                src_ref=acc.at[which, pl.ds(pl.multiple_of(r * N1L, N1L), N1L)],
-                dst_ref=out.at[row], send_sem=s5.at[which], recv_sem=r5.at[which],
+                src_ref=acc.at[which, pl.ds(pl.multiple_of(r * N1L, N1L), N1L), lanes],
+                dst_ref=out.at[row, :, lanes], send_sem=s5.at[unit], recv_sem=r5.at[unit],
                 device_id=(r, col), device_id_type=MESH,
             ).start()
 
@@ -397,19 +425,39 @@
     pltpu.make_async_copy(other_rows, other_rows, s1).wait()
     others = bsend.at[pl.ds(0, DEVS - 1)]
     pltpu.make_async_copy(others, others, s2).wait()
-    for which, out in ((0, oh_ref), (1, ox_ref)):
-        others = tsend.at[which, pl.ds(0, DEVS - 1)]
-        pltpu.make_async_copy(others, others, s4.at[which]).wait()
-        other_rows = acc.at[which, pl.ds(0, (ROWS - 1) * N1L)]
-        pltpu.make_async_copy(other_rows, other_rows, s5.at[which]).wait()
-        pltpu.make_async_copy(out, out, r5.at[which]).wait()
+    for unit, (which, lanes) in enumerate(UNITS):
+        others = tsend.at[which, pl.ds(0, DEVS - 1), :, :, lanes]
+        pltpu.make_async_copy(others, others, s4.at[unit]).wait()
+        other_rows = acc.at[which, pl.ds(0, (ROWS - 1) * N1L), lanes]
+        pltpu.make_async_copy(other_rows, other_rows, s5.at[unit]).wait()
+        out = (oh_ref, ox_ref)[which].at[:, :, lanes]
+        pltpu.make_async_copy(out, out, r5.at[unit]).wait()
+
+
+def hand_over(a_ref, b_ref, c_ref, d_ref, held, in_sem, out_sem):
+    pieces = [
+        (n, pl.ds(4 * k, 4), source, target)
+        for n, (source, target) in enumerate(((a_ref, c_ref), (b_ref, d_ref)))
+        for k in range(4)
+    ]
+    copies = []
+    for k, (n, at, source, _) in enumerate(pieces):
+        copies.append(pltpu.make_async_copy(source.at[at], held.at[n, at], in_sem.at[k]))
+        copies[-1].start()
+    back = []
+    for k, (n, at, _, target) in enumerate(pieces):
+        copies[k].wait()
+        back.append(pltpu.make_async_copy(held.at[n, at], target.at[at], out_sem.at[k]))
+        back[-1].start()
+    for copy in back:
+        copy.wait()
 
 
 def local(grad_out, input_spectrum, filter_spectrum):
     first, last, inner, place = (jnp.asarray(t) for t in tables())
     out = jax.ShapeDtypeStruct((CH, N1L, B), F32)
     dma = pltpu.SemaphoreType.DMA
-    return pl.pallas_call(
+    results = pl.pallas_call(
         kernel,
         out_shape=(out, out),
         in_specs=[pl.BlockSpec(memory_space=pl.ANY)] * 7,
@@ -437,13 +485,20 @@
             dma((6,)),
             dma, dma,
             dma, dma((GROUPS,)),
-            dma((2,)), dma((2, GROUPS)),
-            dma((2,)), dma((2,)),
+            dma((len(UNITS),)), dma((len(UNITS), GROUPS)),
+            dma((len(UNITS),)), dma((len(UNITS),)),
         ],
         compiler_params=pltpu.CompilerParams(
             collective_id=0, has_side_effects=True, vmem_limit_bytes=56 * 2**20
         ),
     )(grad_out, input_spectrum, filter_spectrum, first, last, inner, place)
+    return pl.pallas_call(
+        hand_over,
+        out_shape=(out, out),
+        in_specs=[pl.BlockSpec(memory_space=pl.ANY)] * 2,
+        out_specs=(pl.BlockSpec(memory_space=pl.ANY),) * 2,
+        scratch_shapes=[pltpu.VMEM((2, CH, N1L, B), F32), dma((8,)), dma((8,))],
+    )(*results)
 
 
 def solution(mesh):

time: 118 us -> 107 us (0.907)
  Pallas kernels: 114 us -> 106 us
  local copies, waits for them, and re-layouts: 3.76 us -> 0 us
    pallas_call x1, Pallas kernels: 114 us -> 104 us  [local(): pl.pallas_call(kernel, out_shape=(out, out), in_specs=[pl.BlockSpec(memor...]
    unnamed x2 -> x0, local copies, waits for them, and re-layouts: 3.76 us -> none
    pallas_call x0 -> x1, Pallas kernels: none -> 2.09 us  [local(): pl.pallas_call(hand_over, out_shape=(out, out), in_specs=[pl.BlockSpec(me...]
where the time goes in v2:
time: 107 us
  Pallas kernels  106 us (99%)
    pallas_call x1, Pallas kernels, local(): pl.pallas_call(kernel, out_shape=(out, out), in_specs=[pl.BlockSpec(memor...  104 us

profile of v2, /device:TPU:1, one launch (start us, length us, event | category | flops | bytes accessed | tf_op | source)
XLA Modules:
  0.0 106.6 jit_solution(5309251818484361406)
XLA Ops:
  0.6 103.9 %shard_map.86 = (f32[16,32,256]{2,1,0:T(8,128)}, f32[16,32,256]{2,1,0:T(8,128)}) custom-call(f32[16,32,256]{2,1,0:T(8,128)} %grad_ref.1, f32[2,16,8,2048]{3,2,1,0:T(8,128)} %sx_ref.1, f32[2,16,8,2048]{3,2,1,0:T(8,128)} %sh_ref.1, bf16[2,2048,512]{2,1,0:T(8,128)(2,1)} %constant.8.clone.first_ref, bf16[2,16,512,128]{3,2,1,0:T(8,128)(2,1)} %constant.9.clone.last_ref, ...), custom_call_target="tpu_custom_call" | custom-call | tf_op jit(solution)/shard_map/pallas_call | solution.py:460
  104.5 2.1 %shard_map.87 = (f32[16,32,256]{2,1,0:T(8,128)}, f32[16,32,256]{2,1,0:T(8,128)}) custom-call(f32[16,32,256]{2,1,0:T(8,128)} %get-tuple-element.4.a_ref, f32[16,32,256]{2,1,0:T(8,128)} %get-tuple-element.5.b_ref), custom_call_target="tpu_custom_call" | custom-call | tf_op jit(solution)/shard_map/pallas_call | solution.py:495

commit v3 on v2

--- a/solution.py
+++ b/solution.py
@@ -25,6 +25,7 @@
 RAD = 8
 GROUPS, PER = 4, 4
 UNITS = ((0, pl.ds(0, B)), (1, pl.ds(0, B // 2)), (1, pl.ds(B // 2, B // 2)))
+HALVES = (pl.ds(0, B // 2), pl.ds(B // 2, B // 2))
 ROOT_HALF = float(np.sqrt(0.5))
 
 
@@ -135,9 +136,10 @@
     least = jnp.where(q == 0, 1, 0)
     count = PER * COLS - least
     start = (row * COLS + col) * 29
+    mult = 2 * lax.rem((row * COLS + col) * 7, 15) + 1
 
     def step(i):
-        e = least + lax.rem(i * 13 + start, count)
+        e = least + lax.rem(i * mult + start, count)
         send(row_at(row, q, lax.rem(e, PER), way), col_at(col, lax.div(e, PER)))
 
     loop(0, count, step)
@@ -146,7 +148,7 @@
 def kernel(
     grad_ref, sx_ref, sh_ref, first_ref, last_ref, inner_ref, place_ref,
     oh_ref, ox_ref,
-    raw, spec, first, last, inner, place, xg, xs, bsend, brecv, va, vt,
+    raw, xin, spec, first, last, inner, place, xg, xs, bsend, brecv, va, vt,
     ah, al, us, vs, tsend, trecv, acc,
     lsem, s1, r1, s2, r2, s4, r4, s5, r5,
 ):
@@ -170,6 +172,8 @@
         pl.semaphore_signal(barrier, inc=1, device_id=(row, c), device_id_type=MESH)
     loop(1, ROWS, greet)
 
+    load_x = pltpu.make_async_copy(grad_ref, xin, lsem.at[6])
+    load_x.start()
     loads = [
         pltpu.make_async_copy(sh_ref, raw.at[0], lsem.at[0]),
         pltpu.make_async_copy(sx_ref, raw.at[1], lsem.at[1]),
@@ -201,17 +205,19 @@
     pl.semaphore_wait(barrier, DEVS - 1)
 
     own_rows = pl.ds(pl.multiple_of(row * N1L, N1L), N1L)
-    own_x = pltpu.make_async_copy(grad_ref.at[row], xg.at[own_rows], r1)
-    own_x.start()
-
-    def send_x(i):
-        r = lax.rem(row + i, ROWS)
-        pltpu.make_async_remote_copy(
-            src_ref=grad_ref.at[r], dst_ref=xg.at[own_rows], send_sem=s1, recv_sem=r1,
-            device_id=(r, col), device_id_type=MESH,
-        ).start()
-
-    loop(1, ROWS, send_x)
+    load_x.wait()
+    for h, lanes in enumerate(HALVES):
+        pltpu.make_async_copy(xin.at[row, :, lanes], xg.at[own_rows, lanes], r1.at[h]).start()
+
+        def send_x(i):
+            r = row + i
+            r = jnp.where(r >= ROWS, r - ROWS, r)
+            pltpu.make_async_remote_copy(
+                src_ref=xin.at[r, :, lanes], dst_ref=xg.at[own_rows, lanes], send_sem=s1,
+                recv_sem=r1.at[h], device_id=(r, col), device_id_type=MESH,
+            ).start()
+
+        loop(1, ROWS, send_x)
 
     for load in loads[:3]:
         load.wait()
@@ -255,34 +261,38 @@
     loop(0, 16, order)
 
     loads[3].wait()
-    pltpu.make_async_copy(xg, xg, r1).wait()
-    high, low = split(xg[...])
-    xs[0] = high
-    xs[1] = low
-
-    def first_group(q):
-        rows = [row_at(row, q, m, 1) for m in range(PER)]
-        at = [pl.ds(pl.multiple_of(r * 128, 128), 128) for r in rows]
-        wh = jnp.concatenate([first[0, a] for a in at], axis=0)
-        wl = jnp.concatenate([first[1, a] for a in at], axis=0)
-        value = mm3(wh, wl, xs[0], xs[1])
-        for m in range(PER):
-            block = value[m * 128 : (m + 1) * 128].reshape(COLS, 2, K1L, B)
-            bsend[pl.ds(rows[m] * COLS, COLS)] = block
-
-        @pl.when(q == 0)
-        def _():
-            pltpu.make_async_copy(bsend.at[me], brecv.at[me], r2.at[q]).start()
-
-        def send(r, c):
-            pltpu.make_async_remote_copy(
-                src_ref=bsend.at[r * COLS + c], dst_ref=brecv.at[me], send_sem=s2,
-                recv_sem=r2.at[q], device_id=(r, c), device_id_type=MESH,
-            ).start()
-
-        spread(row, col, q, 1, send)
-
-    loop(0, GROUPS, first_group)
+    for h, lanes in enumerate(HALVES):
+        arrived = xg.at[:, lanes]
+        pltpu.make_async_copy(arrived, arrived, r1.at[h]).wait()
+        high, low = split(xg[:, lanes])
+        xs[0, h] = high
+        xs[1, h] = low
+
+        def first_group(q):
+            rows = [row_at(row, q, m, 1) for m in range(PER)]
+            at = [pl.ds(pl.multiple_of(r * 128, 128), 128) for r in rows]
+            wh = jnp.concatenate([first[0, a] for a in at], axis=0)
+            wl = jnp.concatenate([first[1, a] for a in at], axis=0)
+            value = mm3(wh, wl, xs[0, h], xs[1, h])
+            for m in range(PER):
+                block = value[m * 128 : (m + 1) * 128].reshape(COLS, 2, K1L, B // 2)
+                bsend[pl.ds(rows[m] * COLS, COLS), :, :, lanes] = block
+
+            @pl.when(q == 0)
+            def _():
+                pltpu.make_async_copy(
+                    bsend.at[me, :, :, lanes], brecv.at[me, :, :, lanes], r2.at[q]
+                ).start()
+
+            def send(r, c):
+                pltpu.make_async_remote_copy(
+                    src_ref=bsend.at[r * COLS + c, :, :, lanes], dst_ref=brecv.at[me, :, :, lanes],
+                    send_sem=s2, recv_sem=r2.at[q], device_id=(r, c), device_id_type=MESH,
+                ).start()
+
+            spread(row, col, q, 1, send)
+
+        loop(0, GROUPS, first_group)
 
     loads[4].wait()
 
@@ -388,15 +398,22 @@
     for unit, (which, lanes) in enumerate(UNITS):
         out = (oh_ref, ox_ref)[which]
 
-        def last_group(q):
+        def gathered(q):
             group = trecv.at[which, pl.ds(0, PER * COLS), :, :, lanes]
             pltpu.make_async_copy(group, group, r4.at[unit, q]).wait()
             rows = [row_at(row, q, m, 1) for m in range(PER)]
             parts = [trecv[which, pl.ds(r * COLS, COLS), :, :, lanes] for r in rows]
-            high, low = split(jnp.concatenate([p.reshape(128, p.shape[-1]) for p in parts], axis=0))
-            wh = jnp.concatenate([last[0, r] for r in rows], axis=1)
-            wl = jnp.concatenate([last[1, r] for r in rows], axis=1)
-            value = mm3(wh, wl, high, low)
+            whole = jnp.concatenate([p.reshape(128, p.shape[-1]) for p in parts], axis=0)
+            return rows, *split(whole)
+
+        def added(rows, at, high, low):
+            wh = jnp.concatenate([last[0, r, at] for r in rows], axis=1)
+            wl = jnp.concatenate([last[1, r, at] for r in rows], axis=1)
+            return mm3(wh, wl, high, low)
+
+        def last_group(q):
+            rows, high, low = gathered(q)
+            value = added(rows, pl.ds(0, HALF1), high, low)
 
             @pl.when(q == 0)
             def _():
@@ -406,20 +423,32 @@
             def _():
                 acc[which, :, lanes] += value
 
-        loop(0, GROUPS, last_group)
-        pltpu.make_async_copy(
-            acc.at[which, own_rows, lanes], out.at[row, :, lanes], r5.at[unit]
-        ).start()
-
-        def send_out(i):
-            r = lax.rem(row + i, ROWS)
-            pltpu.make_async_remote_copy(
-                src_ref=acc.at[which, pl.ds(pl.multiple_of(r * N1L, N1L), N1L), lanes],
-                dst_ref=out.at[row, :, lanes], send_sem=s5.at[unit], recv_sem=r5.at[unit],
-                device_id=(r, col), device_id_type=MESH,
-            ).start()
-
-        loop(1, ROWS, send_out)
+        loop(0, GROUPS - 1, last_group)
+
+        rows, high, low = gathered(GROUPS - 1)
+
+        def finish(k):
+            half = lax.rem(lax.div(row, ROWS // 2) + k, 2)
+            at = pl.ds(pl.multiple_of(half * (HALF1 // 2), HALF1 // 2), HALF1 // 2)
+            acc[which, at, lanes] += added(rows, at, high, low)
+
+            @pl.when(k == 0)
+            def _():
+                pltpu.make_async_copy(
+                    acc.at[which, own_rows, lanes], out.at[row, :, lanes], r5.at[unit]
+                ).start()
+
+            def send_out(i):
+                r = half * (ROWS // 2) + lax.rem(row + i, ROWS // 2)
+                pltpu.make_async_remote_copy(
+                    src_ref=acc.at[which, pl.ds(pl.multiple_of(r * N1L, N1L), N1L), lanes],
+                    dst_ref=out.at[row, :, lanes], send_sem=s5.at[unit], recv_sem=r5.at[unit],
+                    device_id=(r, col), device_id_type=MESH,
+                ).start()
+
+            loop(jnp.where(k == 0, 1, 0), ROWS // 2, send_out)
+
+        loop(0, 2, finish)
 
     other_rows = xg.at[pl.ds(0, (ROWS - 1) * N1L)]
     pltpu.make_async_copy(other_rows, other_rows, s1).wait()
@@ -464,13 +493,14 @@
         out_specs=(pl.BlockSpec(memory_space=pl.ANY),) * 2,
         scratch_shapes=[
             pltpu.VMEM((2, 2, CH, K1L, N2), F32),
+            pltpu.VMEM((CH, N1L, B), F32),
             pltpu.VMEM((2, 2, CH, RAD * K1L, B), F32),
             pltpu.VMEM((2, 2 * N1, HALF1), BF16),
             pltpu.VMEM((2, ROWS, HALF1, 128), BF16),
             pltpu.VMEM((4, 2 * B, 2 * B), BF16),
             pltpu.VMEM((B, B), BF16),
             pltpu.VMEM((HALF1, B), F32),
-            pltpu.VMEM((2, HALF1, B), BF16),
+            pltpu.VMEM((2, 2, HALF1, B // 2), BF16),
             pltpu.VMEM((DEVS, 2, K1L, B), F32),
             pltpu.VMEM((DEVS, 2, K1L, B), F32),
             pltpu.VMEM((2, RAD, K1L, B), F32),
@@ -482,8 +512,8 @@
             pltpu.VMEM((2, DEVS, 2, K1L, B), F32),
             pltpu.VMEM((2, DEVS, 2, K1L, B), F32),
             pltpu.VMEM((2, HALF1, B), F32),
-            dma((6,)),
-            dma, dma,
+            dma((7,)),
+            dma, dma((2,)),
             dma, dma((GROUPS,)),
             dma((len(UNITS),)), dma((len(UNITS), GROUPS)),
             dma((len(UNITS),)), dma((len(UNITS),)),

time: 107 us -> 105 us (0.981)
  Pallas kernels: 106 us -> 104 us
    pallas_call x1, Pallas kernels: 104 us -> 102 us  [local(): pl.pallas_call(kernel, out_shape=(out, out), in_specs=[pl.BlockSpec(memor...]
where the time goes in v3:
time: 105 us
  Pallas kernels  104 us (99%)
    pallas_call x1, Pallas kernels, local(): pl.pallas_call(kernel, out_shape=(out, out), in_specs=[pl.BlockSpec(memor...  102 us

profile of v3, /device:TPU:1, one launch (start us, length us, event | category | flops | bytes accessed | tf_op | source)
XLA Modules:
  0.0 104.7 jit_solution(2466178848149904939)
XLA Ops:
  0.6 102.0 %shard_map.86 = (f32[16,32,256]{2,1,0:T(8,128)}, f32[16,32,256]{2,1,0:T(8,128)}) custom-call(f32[16,32,256]{2,1,0:T(8,128)} %grad_ref.1, f32[2,16,8,2048]{3,2,1,0:T(8,128)} %sx_ref.1, f32[2,16,8,2048]{3,2,1,0:T(8,128)} %sh_ref.1, bf16[2,2048,512]{2,1,0:T(8,128)(2,1)} %constant.8.clone.first_ref, bf16[2,16,512,128]{3,2,1,0:T(8,128)(2,1)} %constant.9.clone.last_ref, ...), custom_call_target="tpu_custom_call" | custom-call | tf_op jit(solution)/shard_map/pallas_call | solution.py:489
  102.6 2.1 %shard_map.87 = (f32[16,32,256]{2,1,0:T(8,128)}, f32[16,32,256]{2,1,0:T(8,128)}) custom-call(f32[16,32,256]{2,1,0:T(8,128)} %get-tuple-element.4.a_ref, f32[16,32,256]{2,1,0:T(8,128)} %get-tuple-element.5.b_ref), custom_call_target="tpu_custom_call" | custom-call | tf_op jit(solution)/shard_map/pallas_call | solution.py:525

commit v4 on v3

--- a/solution.py
+++ b/solution.py
@@ -24,7 +24,7 @@
 B = N2 // COLS
 RAD = 8
 GROUPS, PER = 4, 4
-UNITS = ((0, pl.ds(0, B)), (1, pl.ds(0, B // 2)), (1, pl.ds(B // 2, B // 2)))
+UNITS = ((0, pl.ds(0, B)), (1, pl.ds(0, B)))
 HALVES = (pl.ds(0, B // 2), pl.ds(B // 2, B // 2))
 ROOT_HALF = float(np.sqrt(0.5))
 
@@ -133,16 +133,18 @@
 
 
 def spread(row, col, q, way, send):
-    least = jnp.where(q == 0, 1, 0)
-    count = PER * COLS - least
-    start = (row * COLS + col) * 29
-    mult = 2 * lax.rem((row * COLS + col) * 7, 15) + 1
-
-    def step(i):
-        e = least + lax.rem(i * mult + start, count)
-        send(row_at(row, q, lax.rem(e, PER), way), col_at(col, lax.div(e, PER)))
-
-    loop(0, count, step)
+    turn = row + col + lax.div(row, 4)
+    rows = [row_at(row, q, lax.rem(m + turn, PER), way) for m in range(PER)]
+    step = 2 * lax.rem(row, 4) + 1
+    start = row * 3 + col * 5 + lax.div(row, 4)
+
+    def visit(i):
+        base = i * step + start
+        for m, r in enumerate(rows):
+            c = lax.rem(base + 3 * m, COLS)
+            pl.when((r != row) | (c != col))(functools.partial(send, r, c))
+
+    loop(0, COLS, visit)
 
 
 def kernel(
@@ -209,18 +211,18 @@
     for h, lanes in enumerate(HALVES):
         pltpu.make_async_copy(xin.at[row, :, lanes], xg.at[own_rows, lanes], r1.at[h]).start()
 
-        def send_x(i):
-            r = row + i
-            r = jnp.where(r >= ROWS, r - ROWS, r)
-            pltpu.make_async_remote_copy(
-                src_ref=xin.at[r, :, lanes], dst_ref=xg.at[own_rows, lanes], send_sem=s1,
-                recv_sem=r1.at[h], device_id=(r, col), device_id_type=MESH,
-            ).start()
-
-        loop(1, ROWS, send_x)
-
-    for load in loads[:3]:
-        load.wait()
+        def send_x(n):
+            r = 2 * lax.rem(lax.div(row, 2) + lax.rem(n, ROWS // 2), ROWS // 2) + lax.div(n, ROWS // 2)
+
+            @pl.when(r != row)
+            def _():
+                pltpu.make_async_remote_copy(
+                    src_ref=xin.at[r, :, lanes], dst_ref=xg.at[own_rows, lanes], send_sem=s1,
+                    recv_sem=r1.at[h], device_id=(r, col), device_id_type=MESH,
+                ).start()
+
+        loop(0, ROWS, send_x)
+
     lane128 = lax.broadcasted_iota(jnp.int32, (16, 128), 1)
 
     def order(n):
@@ -258,7 +260,6 @@
                     spec[which, part, c0 + c, t * 8 : t * 8 + 8, 0:128] = total[0:8]
                     spec[which, part, c0 + c, t * 8 : t * 8 + 8, 128:256] = total[8:16]
 
-    loop(0, 16, order)
 
     loads[3].wait()
     for h, lanes in enumerate(HALVES):
@@ -294,6 +295,9 @@
 
         loop(0, GROUPS, first_group)
 
+    for load in loads[:3]:
+        load.wait()
+    loop(0, 16, order)
     loads[4].wait()
 
     def send_back(unit, q):
@@ -391,7 +395,6 @@
 
     loop(0, GROUPS, forward)
     loop(0, GROUPS, second)
-    loop(0, GROUPS, lambda q: send_back(2, q))
 
     loads[5].wait()
 

time: 105 us -> 102 us (0.971)
  Pallas kernels: 104 us -> 102 us
    pallas_call x1, Pallas kernels: 102 us -> 99.4 us  [local(): pl.pallas_call(kernel, out_shape=(out, out), in_specs=[pl.BlockSpec(memor...]
where the time goes in v4:
time: 102 us
  Pallas kernels  102 us (100%)
    pallas_call x1, Pallas kernels, local(): pl.pallas_call(kernel, out_shape=(out, out), in_specs=[pl.BlockSpec(memor...  99.4 us
    pallas_call x1, Pallas kernels, local(): pl.pallas_call(hand_over, out_shape=(out, out), in_specs=[pl.BlockSpec(me...  2.09 us

profile of v4, /device:TPU:1, one launch (start us, length us, event | category | flops | bytes accessed | tf_op | source)
XLA Modules:
  0.0 102.1 jit_solution(12921974595950198402)
XLA Ops:
  0.6 99.4 %shard_map.86 = (f32[16,32,256]{2,1,0:T(8,128)}, f32[16,32,256]{2,1,0:T(8,128)}) custom-call(f32[16,32,256]{2,1,0:T(8,128)} %grad_ref.1, f32[2,16,8,2048]{3,2,1,0:T(8,128)} %sx_ref.1, f32[2,16,8,2048]{3,2,1,0:T(8,128)} %sh_ref.1, bf16[2,2048,512]{2,1,0:T(8,128)(2,1)} %constant.8.clone.first_ref, bf16[2,16,512,128]{3,2,1,0:T(8,128)(2,1)} %constant.9.clone.last_ref, ...), custom_call_target="tpu_custom_call" | custom-call | tf_op jit(solution)/shard_map/pallas_call | solution.py:492
  100.1 2.1 %shard_map.87 = (f32[16,32,256]{2,1,0:T(8,128)}, f32[16,32,256]{2,1,0:T(8,128)}) custom-call(f32[16,32,256]{2,1,0:T(8,128)} %get-tuple-element.4.a_ref, f32[16,32,256]{2,1,0:T(8,128)} %get-tuple-element.5.b_ref), custom_call_target="tpu_custom_call" | custom-call | tf_op jit(solution)/shard_map/pallas_call | solution.py:528

commit v5 on v4

--- a/solution.py
+++ b/solution.py
@@ -184,8 +184,8 @@
         pltpu.make_async_copy(inner_ref, inner, lsem.at[4]),
         pltpu.make_async_copy(last_ref, last, lsem.at[5]),
     ]
-    for load in loads:
-        load.start()
+    for n in (3, 0, 1, 2, 4, 5):
+        loads[n].start()
 
     k1 = me * K1L + lax.broadcasted_iota(jnp.int32, (K1L, B), 0)
     lane = lax.broadcasted_iota(jnp.int32, (K1L, B), 1)
@@ -201,8 +201,6 @@
         angle = phase.astype(F32) * (2.0 * np.pi / TOTAL)
         vt[0, a] = jnp.cos(angle)
         vt[1, a] = jnp.sin(angle)
-
-    loop(0, RAD, turn)
 
     pl.semaphore_wait(barrier, DEVS - 1)
 
@@ -295,6 +293,7 @@
 
         loop(0, GROUPS, first_group)
 
+    loop(0, RAD, turn)
     for load in loads[:3]:
         load.wait()
     loop(0, 16, order)

time: 102 us -> 102 us (level)
  no operation moved by 1% of the time
where the time goes in v5:
time: 102 us
  Pallas kernels  102 us (100%)
    pallas_call x1, Pallas kernels, local(): pl.pallas_call(kernel, out_shape=(out, out), in_specs=[pl.BlockSpec(memor...  99.4 us
    pallas_call x1, Pallas kernels, local(): pl.pallas_call(hand_over, out_shape=(out, out), in_specs=[pl.BlockSpec(me...  2.09 us

profile of v5, /device:TPU:1, one launch (start us, length us, event | category | flops | bytes accessed | tf_op | source)
XLA Modules:
  0.0 102.1 jit_solution(7888448366437530431)
XLA Ops:
  0.6 99.4 %shard_map.86 = (f32[16,32,256]{2,1,0:T(8,128)}, f32[16,32,256]{2,1,0:T(8,128)}) custom-call(f32[16,32,256]{2,1,0:T(8,128)} %grad_ref.1, f32[2,16,8,2048]{3,2,1,0:T(8,128)} %sx_ref.1, f32[2,16,8,2048]{3,2,1,0:T(8,128)} %sh_ref.1, bf16[2,2048,512]{2,1,0:T(8,128)(2,1)} %constant.8.clone.first_ref, bf16[2,16,512,128]{3,2,1,0:T(8,128)(2,1)} %constant.9.clone.last_ref, ...), custom_call_target="tpu_custom_call" | custom-call | tf_op jit(solution)/shard_map/pallas_call | solution.py:491
  100.1 2.1 %shard_map.87 = (f32[16,32,256]{2,1,0:T(8,128)}, f32[16,32,256]{2,1,0:T(8,128)}) custom-call(f32[16,32,256]{2,1,0:T(8,128)} %get-tuple-element.4.a_ref, f32[16,32,256]{2,1,0:T(8,128)} %get-tuple-element.5.b_ref), custom_call_target="tpu_custom_call" | custom-call | tf_op jit(solution)/shard_map/pallas_call | solution.py:527
